TPU v7x, 32 devices: a whole 2x2x4 slice. The times are simulated.
32 devices in a mesh: groups: 2 (over y), pool: 4 (over z), tp: 4 (over x, core).
Axes of the slice: x: 2, y: 2, z: 4, core: 2. Of those that a mesh axis runs over, the one named last changes fastest.
Arguments:
- span_q: bfloat16 [128, 32, 4096], P(('groups', 'pool'), None, 'tp'), parts along dimension 0, may hold values from -200 to 200
- span_kv: bfloat16 [128, 2, 32, 1024], P(('groups', 'pool'), None, None, 'tp'), parts along dimension 0, may hold values from -6 to 6
- span_offset: int32 [128], P(('groups', 'pool')), parts along dimension 0, may hold values from 0 to 2048, as said below
- span_length: int32 [128], P(('groups', 'pool')), parts along dimension 0, may hold values from 1 to 32, as said below
- span_dest: int32 [128], P(('groups', 'pool')), parts along dimension 0, may hold values from 0 to 3, as said below
- prefix_kv: bfloat16 [128, 2, 128, 1024], P(('groups', 'pool'), None, None, 'tp'), parts along dimension 0, may hold values from -6 to 6
- resident_kv: bfloat16 [64, 2, 512, 1024], P(('groups', 'pool'), None, None, 'tp'), parts along dimension 0, may hold values from -6 to 6
- seq_length: int32 [64], P(('groups', 'pool')), parts along dimension 0, may hold values from 1 to 512, as said below
- decode_q: bfloat16 [64, 4, 4096], P(('groups', 'pool'), None, 'tp'), parts along dimension 0, may hold values from -200 to 200
- decode_kv: bfloat16 [64, 2, 4, 1024], P(('groups', 'pool'), None, None, 'tp'), parts along dimension 0, may hold values from -6 to 6
- block_target: int32 [128], P(('groups', 'pool')), parts along dimension 0, may hold values from 0 to 31, as said below
Outputs:
- prefill_out: bfloat16 [128, 32, 4096], P(('groups', 'pool'), None, 'tp'), parts along dimension 0
- decode_out: bfloat16 [64, 4, 4096], P(('groups', 'pool'), None, 'tp'), parts along dimension 0
There are 2 independent parts, one for each index of `groups`. A program takes and returns all parts, laid end to end along the dimension named above; each array names one. Nothing has to cross between parts.
Inputs may be any that keep to these rules, and one draw needn't show every extreme that they name: `span_dest`: the 16 spans of one device name at most 4 spans for any one instance; in every draw some instance gets exactly 4 spans from every device. `span_offset`: 2048 is reached in every draw. `span_length`: 32 is reached in every draw. `seq_length`: 512 is reached in every draw. `block_target`: sequence g belongs to owner g // 8. The 16 blocks of one device name at most 4 blocks for any one owner; in every draw some owner gets exactly 4 blocks from every device.
All inputs are finite; a program needn't handle non-finite values.
Results may differ from a plain program's by a relative error of at most 0.0045.
Values may be sent and summed in bfloat16 or wider, within the bound.
A program may use at most 64 MiB of HBM per device.

v0:
```python
import math

import jax
import jax.numpy as jnp
from jax import lax
from jax.sharding import PartitionSpec as P

HD = 128


masked_low = -1e30


def softmax_parts(scores, allowed):
    masked = jnp.where(allowed, scores, masked_low)
    highest = jnp.max(masked, axis=-1)
    expons = jnp.where(allowed, jnp.exp(masked - highest[..., None]), 0.0)
    return (highest, expons, jnp.sum(expons, axis=-1))


def slot_layout(owners, pool_count, capacity):
    ordinal = jnp.arange(owners.shape[0], dtype=jnp.int32)
    earlier = (owners[None, :] == owners[:, None]) & (ordinal[None, :] < ordinal[:, None])
    ranking = jnp.sum(earlier.astype(jnp.int32), axis=1)
    placed = owners * capacity + ranking
    slot_ids = jnp.arange(pool_count * capacity, dtype=jnp.int32)
    matches = (placed[None, :] == slot_ids[:, None]).astype(jnp.int32)
    source = jnp.dot(matches, ordinal + 1) - 1
    return (placed, source)


def span_attention(query_block, pair_block, meta_block, prefix_keys, prefix_values):
    scaling = HD ** (-0.5)
    prefix_len = prefix_keys.shape[0]
    row_count = query_block.shape[1]
    pref_scores = (
        jnp.einsum("rikgd,jkd->rkgij", query_block, prefix_keys, preferred_element_type=jnp.float32)
        * scaling
    )
    self_scores = (
        jnp.einsum(
            "rikgd,rjkd->rkgij", query_block, pair_block[:, 0], preferred_element_type=jnp.float32
        )
        * scaling
    )
    scores = jnp.concatenate([pref_scores, self_scores], axis=-1)
    offsets = meta_block[:, 0]
    lengths = meta_block[:, 1]
    position = jnp.arange(prefix_len + row_count)
    row_index = jnp.arange(row_count)
    in_span = position - prefix_len
    allowed = jnp.where(
        position[None, None, :] < prefix_len,
        position[None, None, :] < offsets[:, None, None],
        (in_span[None, None, :] <= row_index[None, :, None])
        & (in_span[None, None, :] < lengths[:, None, None]),
    )
    highest, expons, totals = softmax_parts(scores, allowed[:, None, None])
    weights = expons.astype(jnp.bfloat16)
    blended = jnp.einsum(
        "rkgij,jkd->rikgd",
        weights[..., :prefix_len],
        prefix_values,
        preferred_element_type=jnp.float32,
    )
    blended = blended + jnp.einsum(
        "rkgij,rjkd->rikgd",
        weights[..., prefix_len:],
        pair_block[:, 1],
        preferred_element_type=jnp.float32,
    )
    totals = jnp.where(totals > 0, totals, 1.0)
    blended = blended / jnp.transpose(totals, (0, 3, 1, 2))[..., None]
    living = row_index[None, :] < lengths[:, None]
    blended = jnp.where(living[:, :, None, None, None], blended, 0.0)
    return blended.astype(jnp.bfloat16).reshape(query_block.shape[0], row_count, -1)


def value_part(queries, keys, values, allowed):
    scaling = HD ** (-0.5)
    scores = (
        jnp.einsum("stkgd,sjkd->sktgj", queries, keys, preferred_element_type=jnp.float32) * scaling
    )
    highest, expons, totals = softmax_parts(scores, allowed)
    summed = jnp.einsum("sktgj,sjkd->sktgd", expons, values, precision=lax.Precision.HIGHEST)
    return (highest, totals, summed)


def on_device(
    span_q,
    span_kv,
    span_offset,
    span_length,
    span_dest,
    prefix_kv,
    resident_kv,
    seq_length,
    decode_q,
    decode_kv,
    block_target,
):
    pool_count = lax.axis_size("pool")
    span_count, row_count, query_width = span_q.shape
    key_width = span_kv.shape[-1]
    heads = key_width // HD
    sharing = query_width // key_width
    capacity = -(-span_count // pool_count)
    span_slot, span_from = slot_layout(span_dest, pool_count, capacity)
    filled = span_from >= 0
    picked = jnp.maximum(span_from, 0)
    send_q = jnp.where(
        filled[:, None, None], jnp.take(span_q, picked, axis=0), jnp.zeros((), jnp.bfloat16)
    )
    send_pair = jnp.where(
        filled[:, None, None, None], jnp.take(span_kv, picked, axis=0), jnp.zeros((), jnp.bfloat16)
    )
    meta = jnp.stack([span_offset, span_length], axis=1)
    send_meta = jnp.where(filled[:, None], jnp.take(meta, picked, axis=0), 0)
    send_q = send_q.reshape(pool_count, capacity, row_count, query_width)
    send_pair = send_pair.reshape(pool_count, capacity, 2, row_count, key_width)
    send_meta = send_meta.reshape(pool_count, capacity, 2)
    prefix_keys = prefix_kv[:, 0].reshape(-1, heads, HD)
    prefix_values = prefix_kv[:, 1].reshape(-1, heads, HD)
    got_q = lax.all_to_all(send_q, "pool", split_axis=0, concat_axis=0, tiled=True)
    got_pair = lax.all_to_all(send_pair, "pool", split_axis=0, concat_axis=0, tiled=True)
    got_meta = lax.all_to_all(send_meta, "pool", split_axis=0, concat_axis=0, tiled=True)
    senders = got_q.shape[0]
    per_sender = got_q.shape[1]
    total = senders * per_sender
    stride = math.gcd(total, 4)
    flat_q = got_q.reshape(total // stride, stride, row_count, heads, sharing, HD)
    flat_pair = got_pair.reshape(total // stride, stride, 2, row_count, heads, HD)
    flat_meta = got_meta.reshape(total // stride, stride, 2)

    def one_group(pieces):
        return span_attention(pieces[0], pieces[1], pieces[2], prefix_keys, prefix_values)

    results = lax.map(one_group, (flat_q, flat_pair, flat_meta))
    results = results.reshape(senders, per_sender, row_count, query_width)
    returned = lax.all_to_all(results, "pool", split_axis=0, concat_axis=0, tiled=True)
    returned = returned.reshape(pool_count * capacity, row_count, query_width)
    prefill_out = jnp.take(returned, span_slot, axis=0)
    seqs_here, steps = (decode_q.shape[0], decode_q.shape[1])
    local_ids = lax.axis_index("pool") * seqs_here + jnp.arange(seqs_here, dtype=jnp.int32)
    step_q = decode_q.reshape(seqs_here, steps, heads, sharing, HD)
    res_keys = resident_kv[:, 0].reshape(seqs_here, -1, heads, HD)
    res_values = resident_kv[:, 1].reshape(seqs_here, -1, heads, HD)
    res_allowed = jnp.arange(res_keys.shape[1])[None, :] < seq_length[:, None]
    high_res, total_res, sum_res = value_part(
        step_q, res_keys, res_values, res_allowed[:, None, None, None, :]
    )
    new_keys = decode_kv[:, 0].reshape(seqs_here, steps, heads, HD)
    new_values = decode_kv[:, 1].reshape(seqs_here, steps, heads, HD)
    step_index = jnp.arange(steps)
    new_allowed = step_index[None, :] <= step_index[:, None]
    high_new, total_new, sum_new = value_part(
        step_q, new_keys, new_values, new_allowed[None, None, :, None, :]
    )
    blocks_here, block_len = (prefix_kv.shape[0], prefix_kv.shape[2])
    block_cap = -(-blocks_here // pool_count)
    block_slot, block_from = slot_layout(block_target // seqs_here, pool_count, block_cap)
    block_filled = block_from >= 0
    block_pick = jnp.maximum(block_from, 0)
    slot_target = jnp.where(block_filled, jnp.take(block_target, block_pick), -1).reshape(
        pool_count, block_cap
    )
    slot_pair = jnp.where(
        block_filled[:, None, None, None],
        jnp.take(prefix_kv, block_pick, axis=0),
        jnp.zeros((), jnp.bfloat16),
    )
    slot_pair = slot_pair.reshape(pool_count, block_cap, 2, block_len, key_width)
    got_pair, got_target = (
        lax.all_to_all(slot_pair, "pool", split_axis=0, concat_axis=0, tiled=True),
        lax.all_to_all(slot_target, "pool", split_axis=0, concat_axis=0, tiled=True),
    )
    moved_keys = got_pair[:, :, 0].reshape(-1, heads, HD)
    moved_values = got_pair[:, :, 1].reshape(-1, heads, HD)
    key_owner = jnp.broadcast_to(
        got_target.reshape(-1, 1), (pool_count * block_cap, block_len)
    ).reshape(-1)
    moved_allowed = key_owner[None, :] == local_ids[:, None]
    scaling = HD ** (-0.5)
    scores = (
        jnp.einsum("stkgd,jkd->sktgj", step_q, moved_keys, preferred_element_type=jnp.float32)
        * scaling
    )
    high_mov, expons, total_mov = softmax_parts(scores, moved_allowed[:, None, None, None, :])
    sum_mov = jnp.einsum("sktgj,jkd->sktgd", expons, moved_values, precision=lax.Precision.HIGHEST)
    highest = jnp.maximum(jnp.maximum(high_res, high_mov), high_new)
    scale_res = jnp.exp(high_res - highest)
    scale_mov = jnp.exp(high_mov - highest)
    scale_new = jnp.exp(high_new - highest)
    totals = total_res * scale_res + total_mov * scale_mov + total_new * scale_new
    blended = (
        sum_res * scale_res[..., None]
        + sum_mov * scale_mov[..., None]
        + sum_new * scale_new[..., None]
    )
    blended = blended / totals[..., None]
    decode_out = (
        jnp.transpose(blended, (0, 2, 1, 3, 4))
        .astype(jnp.bfloat16)
        .reshape(seqs_here, steps, query_width)
    )
    return (prefill_out, decode_out)


def solution(mesh):
    return jax.shard_map(
        on_device,
        mesh=mesh,
        in_specs=(
            P(("groups", "pool"), None, "tp"),
            P(("groups", "pool"), None, None, "tp"),
            P(("groups", "pool")),
            P(("groups", "pool")),
            P(("groups", "pool")),
            P(("groups", "pool"), None, None, "tp"),
            P(("groups", "pool"), None, None, "tp"),
            P(("groups", "pool")),
            P(("groups", "pool"), None, "tp"),
            P(("groups", "pool"), None, None, "tp"),
            P(("groups", "pool")),
        ),
        out_specs=(P(("groups", "pool"), None, "tp"), P(("groups", "pool"), None, "tp")),
        check_vma=False,
    )
```

profile of v0, /device:TPU:0, one launch (start us, length us, event | category | flops | bytes accessed | tf_op | source)
XLA Modules:
  0.0 175.5 jit_solution(10736959682979414489)
XLA Ops:
  4.4 6.3 %all-to-all-start.4 = ((s32[4,1,4]{2,1,0:T(1,128)}), s32[4,1,4]{2,1,0:T(1,128)S(1)}, u32[]{:S(2)}, u32[]{:S(2)}) async-start(s32[4,1,4]{2,1,0:T(1,128)} %bitcast.34), calls=%async_computation.4 | async-start | bytes 4096 | tf_op jit(solution)/shard_map/all_to_all | solution.py:175
  10.7 3.1 %fusion.81 = (bf16[16,1,128,256]{3,2,1,0:T(8,128)(2,1)}, bf16[16,1,128,256]{3,2,1,0:T(8,128)(2,1)}) fusion(bf16[16,2,128,256]{3,2,1,0:T(8,128)(2,1)} %param.20), kind=kLoop, calls=%fused_computation.154 | loop fusion | bytes 4194304 | tf_op jit(solution)/shard_map/slice | solution.py:123
  13.8 2.3 %gather_fusion.3 = bf16[16,2,128,256]{3,2,1,0:T(8,128)(2,1)S(1)} fusion(bf16[16,2,128,256]{3,2,1,0:T(8,128)(2,1)} %param.20, s32[1024]{0:T(1024)S(1)} %pad_clamp_fusion), kind=kCustom, calls=%fused_computation.5 | custom fusion | bytes 4194368 | tf_op jit(solution)/shard_map/jit(_take)/gather | solution.py:169
  19.7 2.2 %reshape.385 = bf16[2048,2,128]{2,1,0:T(2,128)(2,1)} reshape(bf16[16,1,128,256]{3,2,1,0:T(8,128)(2,1)} %get-tuple-element.181) | data formatting | bytes 2097152 | tf_op jit(solution)/shard_map/reshape;squeeze | solution.py:122
  23.2 2.5 %gather_fusion.1 = bf16[16,2,32,256]{3,2,1,0:T(8,128)(2,1)} fusion(bf16[16,2,32,256]{3,2,1,0:T(8,128)(2,1)} %param.16, s32[1024]{0:T(1024)S(1)} %pad_clamp_fusion.2), kind=kCustom, calls=%fused_computation.3 | custom fusion | bytes 1048640 | tf_op jit(solution)/shard_map/jit(_take)/gather | solution.py:115
  25.7 2.0 %select_select_fusion.2 = bf16[4,4,2,32,256]{4,3,2,1,0:T(8,128)(2,1)} fusion(bf16[4,4,2,32,256]{4,3,2,1,0:T(8,128)(2,1)} %bitcast.235, pred[4,4]{1,0:T(4,128)(4,1)S(1)} %broadcast_in_dim.289, pred[4,4]{1,0:T(4,128)(4,1)S(1)} %broadcast_in_dim.287), kind=kLoop, calls=%fused_computation.79 | loop fusion | flops 524288 | bytes 1048608 | tf_op jit(solution)/shard_map/jit(_where)/select_n | solution.py:114
  27.7 2.2 %reshape.386 = bf16[2048,2,128]{2,1,0:T(2,128)(2,1)} reshape(bf16[16,1,128,256]{3,2,1,0:T(8,128)(2,1)} %get-tuple-element.180) | data formatting | bytes 2097152 | tf_op jit(solution)/shard_map/reshape;squeeze | solution.py:123
  30.0 2.4 %copy.166 = bf16[2048,2,128]{2,0,1:T(8,128)(2,1)} copy(bf16[2048,2,128]{2,1,0:T(2,128)(2,1)} %reshape.386) | data formatting | bytes 2097152 | tf_op jit(solution)/shard_map/while | solution.py:138
  34.3 5.1 %all-to-all-start.2 = ((bf16[4,4,2,32,256]{4,3,2,1,0:T(8,128)(2,1)}), bf16[4,4,2,32,256]{4,3,2,1,0:T(8,128)(2,1)}, u32[]{:S(2)}, u32[]{:S(2)}) async-start(bf16[4,4,2,32,256]{4,3,2,1,0:T(8,128)(2,1)} %select_select_fusion.2), calls=%async_computation.2 | async-start | bytes 1048576 | tf_op jit(solution)/shard_map/all_to_all | solution.py:125
  39.4 4.6 %fusion.79 = (bf16[8,1,512,256]{3,2,1,0:T(8,128)(2,1)}, bf16[8,1,512,256]{3,2,1,0:T(8,128)(2,1)}) fusion(bf16[8,2,512,256]{3,2,1,0:T(8,128)(2,1)} %param.21), kind=kLoop, calls=%fused_computation.152 | loop fusion | bytes 8388608 | tf_op jit(solution)/shard_map/slice | solution.py:147
  44.0 2.9 %copy.216 = bf16[8,1,512,256]{2,3,0,1:T(8,128)(2,1)S(1)} copy(bf16[8,1,512,256]{3,2,1,0:T(8,128)(2,1)} %get-tuple-element.177) | data formatting | bytes 4194304
  46.8 3.9 %copy.217 = bf16[8,1,512,256]{2,3,0,1:T(8,128)(2,1)} copy(bf16[8,1,512,256]{3,2,1,0:T(8,128)(2,1)} %get-tuple-element.176) | data formatting | bytes 4194304
  50.8 2.5 %select_select_fusion.1 = bf16[16,32,1024]{2,1,0:T(8,128)(2,1)} fusion(bf16[16,32,1024]{2,1,0:T(8,128)(2,1)} %gather_fusion.4, pred[16]{0:T(512)(128)(4,1)S(1)} %get-tuple-element.185, pred[16]{0:T(512)(128)(4,1)S(1)} %get-tuple-element.184), kind=kLoop, calls=%fused_computation.76 | loop fusion | flops 1048576 | bytes 2097184 | tf_op jit(solution)/shard_map/jit(_where)/select_n | solution.py:111
  53.4 4.9 %all-to-all-start.1 = ((bf16[4,4,32,1024]{3,2,1,0:T(8,128)(2,1)}), bf16[4,4,32,1024]{3,2,1,0:T(8,128)(2,1)}, u32[]{:S(2)}, u32[]{:S(2)}) async-start(bf16[4,4,32,1024]{3,2,1,0:T(8,128)(2,1)} %bitcast.232), calls=%async_computation.1 | async-start | bytes 2097152 | tf_op jit(solution)/shard_map/all_to_all | solution.py:124
  62.5 20.5 %all-to-all-done.1 = bf16[4,4,32,1024]{3,2,1,0:T(8,128)(2,1)} async-done(((bf16[4,4,32,1024]{3,2,1,0:T(8,128)(2,1)}), bf16[4,4,32,1024]{3,2,1,0:T(8,128)(2,1)}, u32[]{:S(2)}, u32[]{:S(2)}) %all-to-all-start.1) | async-done | bytes 1048608 | tf_op jit(solution)/shard_map/all_to_all | solution.py:124
  83.1 3.2 %all-to-all-start = ((s32[4,4,2]{1,2,0:T(2,128)}), s32[4,4,2]{1,2,0:T(2,128)S(1)}, u32[]{:S(2)}, u32[]{:S(2)}) async-start(s32[4,4,2]{1,2,0:T(2,128)} %copy.160), calls=%async_computation | async-start | bytes 8192 | tf_op jit(solution)/shard_map/all_to_all | solution.py:126
  87.6 1.8 %reshape.308 = bf16[4,4,32,2,4,128]{5,4,3,2,1,0:T(4,128)(2,1)S(1)} reshape(bf16[4,4,32,1024]{3,2,1,0:T(8,128)(2,1)} %all-to-all-done.1) | data formatting | bytes 2097152 | tf_op jit(solution)/shard_map/reshape | solution.py:131
  89.4 2.5 %all-to-all-done = s32[4,4,2]{1,2,0:T(2,128)S(1)} async-done(((s32[4,4,2]{1,2,0:T(2,128)}), s32[4,4,2]{1,2,0:T(2,128)S(1)}, u32[]{:S(2)}, u32[]{:S(2)}) %all-to-all-start) | async-done | bytes 160 | tf_op jit(solution)/shard_map/all_to_all | solution.py:126
  91.9 4.5 %all-to-all-start.5 = ((bf16[4,4,2,128,256]{4,3,1,2,0:T(8,128)(2,1)}), bf16[4,4,2,128,256]{4,3,1,2,0:T(8,128)(2,1)}, u32[]{:S(2)}, u32[]{:S(2)}) async-start(bf16[4,4,2,128,256]{4,3,1,2,0:T(8,128)(2,1)} %copy.173), calls=%async_computation.5 | async-start | bytes 4194304 | tf_op jit(solution)/shard_map/all_to_all | solution.py:174
  96.3 32.8 %while.12 = (s32[]{:T(128)}, bf16[4,4,32,1024]{3,2,1,0:T(8,128)(2,1)}, s32[4,4,2]{1,2,0:T(2,128)S(1)}, bf16[4,4,32,2,4,128]{5,4,3,2,1,0:T(4,128)(2,1)S(1)}, bf16...) while((s32[]{:T(128)}, ...), condition=%wide.region_4.6_spmd, body=%wide.region_1.5_spmd.sunk | while | flops 1106576768 | bytes 37654392 | solution.py:138
  98.5 3.4 %fusion.106 = (f32[4,2,4,32]{3,2,0,1:T(4,128)S(1)}, bf16[4,2,4,32,2080]{4,3,2,0,1:T(8,128)(2,1)S(1)}) fusion(f32[4,2,4,32,32]{4,3,2,0,1:T(8,128)S(1)} %fusion.104, f32[4,2,4,32,2048]{4,3,2,0,1:T(8,128)S(1)} %multiply_bitcast_fusion.2, pred[4,32,2080]{2,1,0:T(8,128)(4,1)S(1)} %and_select_fusion.3), kind=kOutput, calls=%fused_computation.151.clone.1 | output fusion | flops 12781599 | bytes 13049856 | tf_op jit(solution)/shard_map/while/body/eval_jaxpr/sub | solution.py:17
  106.7 3.4 %fusion.106 = (f32[4,2,4,32]{3,2,0,1:T(4,128)S(1)}, bf16[4,2,4,32,2080]{4,3,2,0,1:T(8,128)(2,1)S(1)}) fusion(f32[4,2,4,32,32]{4,3,2,0,1:T(8,128)S(1)} %fusion.104, f32[4,2,4,32,2048]{4,3,2,0,1:T(8,128)S(1)} %multiply_bitcast_fusion.2, pred[4,32,2080]{2,1,0:T(8,128)(4,1)S(1)} %and_select_fusion.3), kind=kOutput, calls=%fused_computation.151.clone.1 | output fusion | flops 12781599 | bytes 13049856 | tf_op jit(solution)/shard_map/while/body/eval_jaxpr/sub | solution.py:17
  114.9 3.4 %fusion.106 = (f32[4,2,4,32]{3,2,0,1:T(4,128)S(1)}, bf16[4,2,4,32,2080]{4,3,2,0,1:T(8,128)(2,1)S(1)}) fusion(f32[4,2,4,32,32]{4,3,2,0,1:T(8,128)S(1)} %fusion.104, f32[4,2,4,32,2048]{4,3,2,0,1:T(8,128)S(1)} %multiply_bitcast_fusion.2, pred[4,32,2080]{2,1,0:T(8,128)(4,1)S(1)} %and_select_fusion.3), kind=kOutput, calls=%fused_computation.151.clone.1 | output fusion | flops 12781599 | bytes 13049856 | tf_op jit(solution)/shard_map/while/body/eval_jaxpr/sub | solution.py:17
  123.1 3.4 %fusion.106 = (f32[4,2,4,32]{3,2,0,1:T(4,128)S(1)}, bf16[4,2,4,32,2080]{4,3,2,0,1:T(8,128)(2,1)S(1)}) fusion(f32[4,2,4,32,32]{4,3,2,0,1:T(8,128)S(1)} %fusion.104, f32[4,2,4,32,2048]{4,3,2,0,1:T(8,128)S(1)} %multiply_bitcast_fusion.2, pred[4,32,2080]{2,1,0:T(8,128)(4,1)S(1)} %and_select_fusion.3), kind=kOutput, calls=%fused_computation.151.clone.1 | output fusion | flops 12781599 | bytes 13049856 | tf_op jit(solution)/shard_map/while/body/eval_jaxpr/sub | solution.py:17
  129.2 13.8 %all-to-all-done.5 = bf16[4,4,2,128,256]{4,3,1,2,0:T(8,128)(2,1)} async-done(((bf16[4,4,2,128,256]{4,3,1,2,0:T(8,128)(2,1)}), bf16[4,4,2,128,256]{4,3,1,2,0:T(8,128)(2,1)}, u32[]{:S(2)}, u32[]{:S(2)}) %all-to-all-start.5) | async-done | bytes 2097184 | tf_op jit(solution)/shard_map/all_to_all | solution.py:174
  142.9 4.4 %all-to-all-start.3 = ((bf16[4,4,32,1024]{3,2,1,0:T(8,128)(2,1)}), bf16[4,4,32,1024]{3,2,1,0:T(8,128)(2,1)}, u32[]{:S(2)}, u32[]{:S(2)}) async-start(bf16[4,4,32,1024]{3,2,1,0:T(8,128)(2,1)} %get-tuple-element.92), calls=%async_computation.3 | async-start | bytes 2097152 | tf_op jit(solution)/shard_map/all_to_all | solution.py:140
  150.2 1.8 %fusion.83 = (f32[8,2,4,4]{0,3,2,1:T(4,128)S(1)}, f32[8,2,4,4,2048]{4,0,3,2,1:T(8,128)S(1)}) fusion(bf16[8,4,2,4,128]{4,3,2,1,0:T(4,128)(2,1)S(1)} %reshape.311, bf16[2048,2,128,1,1]{2,1,0,4,3:T(2,128)(2,1)} %bitcast.233, pred[8,2048]{1,0:T(8,128)(4,1)S(1)} %broadcast_compare_fusion.1), kind=kOutput, calls=%fused_computation.156 | convolution fusion | flops 135790336 | bytes 3228672 | tf_op jit(solution)/shard_map/stkgd,jkd->sktgj/dot_general | solution.py:185
  152.1 1.7 fusion.77
  156.4 4.4 %fusion.35 = f32[8,4,2,4,128]{4,3,1,2,0:T(4,128)S(1)} fusion(f32[8,2,4,4,2048]{4,0,3,2,1:T(8,128)S(1)} %copy-done.3, bf16[2048,2,128,1,1]{2,1,0,4,3:T(2,128)(2,1)} %bitcast.236, f32[8,4,2,4]{3,1,2,0:T(4,128)S(1)} %get-tuple-element.161), kind=kOutput, calls=%fused_computation.66 | convolution fusion | flops 805339136 | bytes 3277824 | tf_op jit(solution)/shard_map/sktgj,jkd->sktgd/dot_general | solution.py:189
  160.8 1.9 %fusion.39 = bf16[8,4,2,4,128]{4,3,1,2,0:T(4,128)(2,1)S(1)} fusion(f32[8,4,2,4,128]{4,3,1,2,0:T(4,128)S(1)} %fusion.34, f32[8,4,2,4,128]{4,3,1,2,0:T(4,128)S(1)} %fusion.35, bf16[8,512,2,128,1]{1,3,4,2,0:T(8,128)(2,1)S(1)} %bitcast.234, f32[8,2,4,4,512]{4,3,2,1,0:T(4,128)S(1)} %copy-done.5, f32[8,2,4,4]{3,2,1,0:T(4,128)S(1)} %get-tuple-element.194, ...), kind=kOutput, calls=%fused_computation.69 | convolution fusion | flops 201752576 | bytes 2956288 | tf_op jit(solution)/shard_map/sktgj,sjkd->sktgd/dot_general | solution.py:85
  163.4 9.0 %all-to-all-done.3 = bf16[4,4,32,1024]{3,2,1,0:T(8,128)(2,1)} async-done(((bf16[4,4,32,1024]{3,2,1,0:T(8,128)(2,1)}), bf16[4,4,32,1024]{3,2,1,0:T(8,128)(2,1)}, u32[]{:S(2)}, u32[]{:S(2)}) %all-to-all-start.3) | async-done | bytes 1048608 | tf_op jit(solution)/shard_map/all_to_all | solution.py:140
  172.5 1.9 %gather_fusion.5 = bf16[16,32,1024]{2,1,0:T(8,128)(2,1)S(1)} fusion(bf16[16,32,1024]{2,1,0:T(8,128)(2,1)} %bitcast.25, s32[1024]{0:T(1024)S(1)} %pad_clamp_fusion.1), kind=kCustom, calls=%fused_computation.1.clone | custom fusion | bytes 2097216 | tf_op jit(solution)/shard_map/jit(_take)/gather | solution.py:142
  (169 shorter events, 42.1 us)
Async XLA Ops:
  0.6 17.5 %copy-start = (bf16[16,32,1024]{2,1,0:T(8,128)(2,1)S(1)}, bf16[16,32,1024]{2,1,0:T(8,128)(2,1)}, u32[]{:S(2)}) copy-start(bf16[16,32,1024]{2,1,0:T(8,128)(2,1)} %param.15) | copy-start | bytes 3145732
  4.4 29.9 %all-to-all-start.4 = ((s32[4,1,4]{2,1,0:T(1,128)}), s32[4,1,4]{2,1,0:T(1,128)S(1)}, u32[]{:S(2)}, u32[]{:S(2)}) async-start(s32[4,1,4]{2,1,0:T(1,128)} %bitcast.34), calls=%async_computation.4 | async-start | bytes 4096 | tf_op jit(solution)/shard_map/all_to_all | solution.py:175
  13.8 2.3 %copy-start.9 = (s32[16]{0:T(128)S(1)}, s32[16]{0:T(128)}, u32[]{:S(2)}) copy-start(s32[16]{0:T(128)} %param.18) | copy-start | bytes 196
  13.8 2.4 %copy-start.10 = (s32[16]{0:T(128)S(1)}, s32[16]{0:T(128)}, u32[]{:S(2)}) copy-start(s32[16]{0:T(128)} %param.17) | copy-start | bytes 196
  13.8 2.5 %copy-start.11 = (s32[16]{0:T(128)S(1)}, s32[16]{0:T(128)}, u32[]{:S(2)}) copy-start(s32[16]{0:T(128)} %param.19) | copy-start | bytes 196
  27.7 4.6 %copy-start.7 = (bf16[8,4,1024]{2,1,0:T(4,128)(2,1)S(1)}, bf16[8,4,1024]{2,1,0:T(4,128)(2,1)}, u32[]{:S(2)}) copy-start(bf16[8,4,1024]{2,1,0:T(4,128)(2,1)} %param.23) | copy-start | bytes 196612
  34.3 19.1 %all-to-all-start.2 = ((bf16[4,4,2,32,256]{4,3,2,1,0:T(8,128)(2,1)}), bf16[4,4,2,32,256]{4,3,2,1,0:T(8,128)(2,1)}, u32[]{:S(2)}, u32[]{:S(2)}) async-start(bf16[4,4,2,32,256]{4,3,2,1,0:T(8,128)(2,1)} %select_select_fusion.2), calls=%async_computation.2 | async-start | bytes 1048576 | tf_op jit(solution)/shard_map/all_to_all | solution.py:125
  50.8 7.6 %copy-start.12 = (bf16[8,2,4,256]{3,2,1,0:T(4,128)(2,1)S(1)}, bf16[8,2,4,256]{3,2,1,0:T(4,128)(2,1)}, u32[]{:S(2)}) copy-start(bf16[8,2,4,256]{3,2,1,0:T(4,128)(2,1)} %param.24) | copy-start | bytes 98308
  50.8 8.5 %copy-start.8 = (s32[8]{0:T(128)S(1)}, s32[8]{0:T(128)}, u32[]{:S(2)}) copy-start(s32[8]{0:T(128)} %param.22) | copy-start | bytes 100
  53.4 29.6 %all-to-all-start.1 = ((bf16[4,4,32,1024]{3,2,1,0:T(8,128)(2,1)}), bf16[4,4,32,1024]{3,2,1,0:T(8,128)(2,1)}, u32[]{:S(2)}, u32[]{:S(2)}) async-start(bf16[4,4,32,1024]{3,2,1,0:T(8,128)(2,1)} %bitcast.232), calls=%async_computation.1 | async-start | bytes 2097152 | tf_op jit(solution)/shard_map/all_to_all | solution.py:124
  59.9 0.8 copy-start.4
  83.1 8.8 %all-to-all-start = ((s32[4,4,2]{1,2,0:T(2,128)}), s32[4,4,2]{1,2,0:T(2,128)S(1)}, u32[]{:S(2)}, u32[]{:S(2)}) async-start(s32[4,4,2]{1,2,0:T(2,128)} %copy.160), calls=%async_computation | async-start | bytes 8192 | tf_op jit(solution)/shard_map/all_to_all | solution.py:126
  91.9 51.1 %all-to-all-start.5 = ((bf16[4,4,2,128,256]{4,3,1,2,0:T(8,128)(2,1)}), bf16[4,4,2,128,256]{4,3,1,2,0:T(8,128)(2,1)}, u32[]{:S(2)}, u32[]{:S(2)}) async-start(bf16[4,4,2,128,256]{4,3,1,2,0:T(8,128)(2,1)} %copy.173), calls=%async_computation.5 | async-start | bytes 4194304 | tf_op jit(solution)/shard_map/all_to_all | solution.py:174
  98.5 3.4 %copy-start.6 = (bf16[2048,2,128]{2,0,1:T(8,128)(2,1)S(1)}, bf16[2048,2,128]{2,0,1:T(8,128)(2,1)}, u32[]{:S(2)}) copy-start(bf16[2048,2,128]{2,0,1:T(8,128)(2,1)} %get-tuple-element.277) | copy-start | bytes 3145732 | tf_op jit(solution)/shard_map/while
  106.7 3.4 %copy-start.6 = (bf16[2048,2,128]{2,0,1:T(8,128)(2,1)S(1)}, bf16[2048,2,128]{2,0,1:T(8,128)(2,1)}, u32[]{:S(2)}) copy-start(bf16[2048,2,128]{2,0,1:T(8,128)(2,1)} %get-tuple-element.277) | copy-start | bytes 3145732 | tf_op jit(solution)/shard_map/while
  114.9 3.4 %copy-start.6 = (bf16[2048,2,128]{2,0,1:T(8,128)(2,1)S(1)}, bf16[2048,2,128]{2,0,1:T(8,128)(2,1)}, u32[]{:S(2)}) copy-start(bf16[2048,2,128]{2,0,1:T(8,128)(2,1)} %get-tuple-element.277) | copy-start | bytes 3145732 | tf_op jit(solution)/shard_map/while
  123.1 3.4 %copy-start.6 = (bf16[2048,2,128]{2,0,1:T(8,128)(2,1)S(1)}, bf16[2048,2,128]{2,0,1:T(8,128)(2,1)}, u32[]{:S(2)}) copy-start(bf16[2048,2,128]{2,0,1:T(8,128)(2,1)} %get-tuple-element.277) | copy-start | bytes 3145732 | tf_op jit(solution)/shard_map/while
  142.9 29.5 %all-to-all-start.3 = ((bf16[4,4,32,1024]{3,2,1,0:T(8,128)(2,1)}), bf16[4,4,32,1024]{3,2,1,0:T(8,128)(2,1)}, u32[]{:S(2)}, u32[]{:S(2)}) async-start(bf16[4,4,32,1024]{3,2,1,0:T(8,128)(2,1)} %get-tuple-element.92), calls=%async_computation.3 | async-start | bytes 2097152 | tf_op jit(solution)/shard_map/all_to_all | solution.py:140
  153.9 2.5 %copy-start.3 = (f32[8,2,4,4,2048]{4,0,3,2,1:T(8,128)S(1)}, f32[8,2,4,4,2048]{4,0,3,2,1:T(8,128)}, u32[]{:S(2)}) copy-start(f32[8,2,4,4,2048]{4,0,3,2,1:T(8,128)} %get-tuple-element.164) | copy-start | bytes 6291460
  156.4 4.5 %copy-start.2 = (bf16[8,1,512,256]{2,3,0,1:T(8,128)(2,1)S(1)}, bf16[8,1,512,256]{2,3,0,1:T(8,128)(2,1)}, u32[]{:S(2)}) copy-start(bf16[8,1,512,256]{2,3,0,1:T(8,128)(2,1)} %copy.217) | copy-start | bytes 6291460
  156.4 4.5 %copy-start.5 = (f32[8,2,4,4,512]{4,3,2,1,0:T(4,128)S(1)}, f32[8,2,4,4,512]{4,3,2,1,0:T(4,128)}, u32[]{:S(2)}) copy-start(f32[8,2,4,4,512]{4,3,2,1,0:T(4,128)} %copy-done.4) | copy-start | bytes 1572868
  172.5 3.1 %copy-start.1 = (bf16[16,32,1024]{2,1,0:T(8,128)(2,1)S(1)}, bf16[16,32,1024]{2,1,0:T(8,128)(2,1)}, u32[]{:S(2)}) copy-start(bf16[16,32,1024]{2,1,0:T(8,128)(2,1)} %param.15) | copy-start | bytes 3145732
where the time goes:
time: 177 us; the launch traced here: 176 us
  local copies, waits for them, and re-layouts  50.7 us (29%)
  waiting for transfers between devices  46 us (26%)
  starting transfers between devices  28.5 us (16%)
  other arithmetic  26.4 us (15%)
  matrix products  22.6 us (13%)
    all_to_all x1, waiting for transfers between devices, on_device(): lax.all_to_all(send_q, 'pool', split_axis=0, concat_axis=0, tiled=True)  20.5 us
    all_to_all x1, waiting for transfers between devices, on_device(): lax.all_to_all(slot_pair, 'pool', split_axis=0, concat_axis=0, tiled=True)  13.8 us
    sub x4, other arithmetic, softmax_parts(): expons = jnp.where(allowed, jnp.exp(masked - highest[..., None]), 0.0)  13.7 us
    all_to_all x1, waiting for transfers between devices, on_device(): lax.all_to_all(results, 'pool', split_axis=0, concat_axis=0, tiled=True)  9.04 us
    unnamed x28, local copies, waits for them, and re-layouts  8.37 us
    all_to_all x1, starting transfers between devices, on_device(): lax.all_to_all(slot_target, 'pool', split_axis=0, concat_axis=0, tiled=True)  6.32 us
    all_to_all x1, starting transfers between devices, on_device(): lax.all_to_all(send_pair, 'pool', split_axis=0, concat_axis=0, tiled=True)  5.09 us
    dot_general x4, matrix products, span_attention(): jnp.einsum('rikgd,jkd->rkgij', query_block, prefix_keys, preferred_elemen...  5.03 us
  transfers between devices with their start and end apart: 6, of which 5 were waited for; matrix products, arithmetic and copies ran while one was open for 52% of the time, Pallas kernels for 0%

commit v1 on v0

v1 whole, which is shorter than its diff:
```python
import functools

import jax
import jax.numpy as jnp
from jax import lax
from jax.experimental import pallas as pl
from jax.experimental.pallas import tpu as pltpu
from jax.sharding import PartitionSpec as P

HD = 128
SCALE = HD ** (-0.5)
LOW = -1e30
GAP = 16
NT = (((1,), (1,)), ((), ()))
NN = (((1,), (0,)), ((), ()))


def split_bf16(x):
    high = x.astype(jnp.bfloat16).astype(jnp.float32)
    rest = x - high
    mid = rest.astype(jnp.bfloat16).astype(jnp.float32)
    return high, mid, rest - mid


def pack_stats(top, total):
    a, b, c = split_bf16(top)
    d, e, _ = split_bf16(total)
    out = a + pltpu.roll(b, GAP, 1) + pltpu.roll(c, 2 * GAP, 1)
    out = out + pltpu.roll(d, 3 * GAP, 1) + pltpu.roll(e, 4 * GAP, 1)
    return out.astype(jnp.bfloat16)


def unpack_stats(packed):
    t = packed.astype(jnp.float32)
    top = t + pltpu.roll(t, 128 - GAP, 1) + pltpu.roll(t, 128 - 2 * GAP, 1)
    total = pltpu.roll(t, 128 - 3 * GAP, 1) + pltpu.roll(t, 128 - 4 * GAP, 1)
    return top, total


def soft(scores):
    top = jnp.max(scores, axis=-1, keepdims=True)
    weights = jnp.exp((scores - top) * SCALE)
    return top, weights.astype(jnp.bfloat16), jnp.sum(weights, axis=-1, keepdims=True)


def kernel(
    n, cap, rows, heads, sharing, steps,
    from_ref, back_ref, offset_ref, length_ref, seqlen_ref,
    target_ref, span_q, span_kv, prefix, resident, decode_q, decode_kv,
    prefill_out, decode_out,
    keys, values, res, own_kv, q_send, q_recv, m_send, m_recv, r_send, r_recv,
    self_acc, self_top, self_total,
    q_ssem, q_rsem, m_ssem, m_rsem, r_ssem, r_rsem, loc_sem,
):
    me = lax.axis_index("pool")
    spans = span_q.shape[0]
    seqs = resident.shape[0]
    per = cap + 1
    width = heads * sharing * HD
    tall = sharing * rows

    def at(step):
        return lax.rem(me + step, n)

    loads = []
    for k in range(heads):
        cols = pl.ds(k * HD, HD)
        loads.append(pltpu.make_async_copy(prefix.at[:, 0, :, cols], keys.at[k], loc_sem.at[2 * k]))
        loads.append(pltpu.make_async_copy(prefix.at[:, 1, :, cols], values.at[k], loc_sem.at[2 * k + 1]))
    own_load = pltpu.make_async_copy(span_kv, own_kv, loc_sem.at[2 * heads])
    res_load = pltpu.make_async_copy(resident, res, loc_sem.at[2 * heads + 1])
    for load in loads:
        load.start()
    own_load.start()
    res_load.start()

    barrier = pltpu.get_barrier_semaphore()

    @pl.loop(1, n)
    def _(d):
        pl.semaphore_signal(barrier, inc=1, device_id={"pool": at(d)}, device_id_type=pl.DeviceIdType.MESH)

    def fill(buf, meta, d):
        @pl.loop(0, cap)
        def _(r):
            pick = from_ref[d * cap + r]
            buf[d * per + r] = span_q[pick]
            meta[d, pl.ds(r, 1), :] = jnp.full((1, 128), offset_ref[pick], jnp.int32)

        buf[d * per + cap] = decode_q[...]

    def q_copy(d, to):
        return pltpu.make_async_remote_copy(
            src_ref=q_send.at[pl.ds(d * per, per)],
            dst_ref=q_recv.at[pl.ds(d * per, per)],
            send_sem=q_ssem.at[d], recv_sem=q_rsem.at[d],
            device_id={"pool": to}, device_id_type=pl.DeviceIdType.MESH,
        )

    def m_copy(d, to):
        return pltpu.make_async_remote_copy(
            src_ref=m_send.at[d], dst_ref=m_recv.at[d],
            send_sem=m_ssem.at[d], recv_sem=m_rsem.at[d],
            device_id={"pool": to}, device_id_type=pl.DeviceIdType.MESH,
        )

    def r_copy(d, to):
        return pltpu.make_async_remote_copy(
            src_ref=r_send.at[pl.ds(d * per, per)],
            dst_ref=r_recv.at[pl.ds(d * per, per)],
            send_sem=r_ssem.at[d], recv_sem=r_rsem.at[d],
            device_id={"pool": to}, device_id_type=pl.DeviceIdType.MESH,
        )

    m_send[...] = jnp.zeros_like(m_send)
    m_recv[0] = jnp.zeros(m_recv.shape[1:], jnp.int32)
    pl.semaphore_wait(barrier, n - 1)

    @pl.loop(1, n)
    def _(d):
        fill(q_send, m_send, d)
        m_copy(d, at(d)).start()
        q_copy(d, at(d)).start()

    fill(q_recv, m_recv, 0)

    lane = lax.broadcasted_iota(jnp.int32, (rows, 128), 1)

    def stacked(block, k):
        base = k * sharing * HD
        return jnp.concatenate(
            [block[:, base + g * HD : base + (g + 1) * HD] for g in range(sharing)], axis=0
        )

    def spread(tops, totals, top, total, k):
        for g in range(sharing):
            h = k * sharing + g
            part = slice(g * rows, (g + 1) * rows)
            tops = jnp.where(lane == h, top[part], tops)
            totals = jnp.where(lane == h, total[part], totals)
        return tops, totals

    def attend(buf, out, slot, bias):
        block = buf[slot]
        tops = totals = jnp.zeros((rows, 128), jnp.float32)
        for k in range(heads):
            query = stacked(block, k)
            key = keys[k].reshape(-1, HD)
            value = values[k].reshape(-1, HD)
            score = lax.dot_general(query, key, NT, preferred_element_type=jnp.float32)
            if bias.shape[0] == 1:
                score = score + bias
            else:
                score = (score.reshape(sharing, rows, -1) + bias[None]).reshape(tall, -1)
            top, weight, total = soft(score)
            acc = lax.dot_general(weight, value, NN, preferred_element_type=jnp.float32)
            for g in range(sharing):
                h = k * sharing + g
                out[slot, :, h * HD : (h + 1) * HD] = acc[g * rows : (g + 1) * rows].astype(jnp.bfloat16)
            tops, totals = spread(tops, totals, top, total, k)
        out[slot, :, width:] = pack_stats(tops, totals)

    tokens = keys.shape[1] * keys.shape[2]
    position = lax.broadcasted_iota(jnp.int32, (1, tokens), 1)

    def chunk(out, d):
        @pl.loop(0, cap)
        def _(r):
            limit = m_recv[d, pl.ds(r, 1), :][:, :1]
            attend(q_recv, out, d * per + r, jnp.where(position < limit, 0.0, LOW))

        source = lax.rem(me - d + n, n)
        seq = source * seqs + lax.broadcasted_iota(jnp.int32, (rows, 1), 0) // steps
        attend(q_recv, out, d * per + cap, jnp.where(target_ref[...] == seq, 0.0, LOW))

    for load in loads:
        load.wait()
    chunk(r_recv, 0)

    own_load.wait()
    row_of = lax.rem(lax.broadcasted_iota(jnp.int32, (tall, rows), 0), rows)
    col_of = lax.broadcasted_iota(jnp.int32, (tall, rows), 1)

    def keep(index, k, acc, tops, totals, top, total):
        for g in range(sharing):
            h = k * sharing + g
            self_acc[index, :, h * HD : (h + 1) * HD] = acc[g * rows : (g + 1) * rows]
        return spread(tops, totals, top, total, k)

    @pl.loop(0, spans)
    def _(j):
        block = span_q[j]
        tops = totals = jnp.zeros((rows, 128), jnp.float32)
        for k in range(heads):
            cols = slice(k * HD, (k + 1) * HD)
            score = lax.dot_general(
                stacked(block, k), own_kv[j, 0, :, cols], NT, preferred_element_type=jnp.float32
            )
            top, weight, total = soft(jnp.where(col_of <= row_of, score, LOW))
            acc = lax.dot_general(weight, own_kv[j, 1, :, cols], NN, preferred_element_type=jnp.float32)
            tops, totals = keep(j, k, acc, tops, totals, top, total)
        self_top[j] = tops
        self_total[j] = totals

    res_load.wait()
    res_len = resident.shape[2]
    slot_of = lax.broadcasted_iota(jnp.int32, (1, res_len), 1)
    row_seq = lax.rem(lax.broadcasted_iota(jnp.int32, (tall, 1), 0), rows) // steps
    tops = totals = jnp.zeros((rows, 128), jnp.float32)
    for k in range(heads):
        cols = slice(k * HD, (k + 1) * HD)
        query = stacked(decode_q[...], k)

        def one(s, carry):
            acc, top, total = carry
            score = lax.dot_general(query, res[s, 0, :, cols], NT, preferred_element_type=jnp.float32)
            score = score + jnp.where(slot_of < seqlen_ref[s], 0.0, LOW)
            top_s, weight, total_s = soft(score)
            acc_s = lax.dot_general(weight, res[s, 1, :, cols], NN, preferred_element_type=jnp.float32)
            here = row_seq == s
            return jnp.where(here, acc_s, acc), jnp.where(here, top_s, top), jnp.where(here, total_s, total)

        zero = jnp.zeros((tall, 1), jnp.float32)
        acc, top, total = lax.fori_loop(0, seqs, one, (jnp.zeros((tall, HD), jnp.float32), zero, zero))
        score = lax.dot_general(query, decode_kv[0, :, cols], NT, preferred_element_type=jnp.float32)
        fits = (col_of // steps == row_of // steps) & (col_of <= row_of)
        top_n, weight, total_n = soft(jnp.where(fits, score, LOW))
        acc_n = lax.dot_general(weight, decode_kv[1, :, cols], NN, preferred_element_type=jnp.float32)
        best = jnp.maximum(top, top_n)
        a = jnp.exp((top - best) * SCALE)
        b = jnp.exp((top_n - best) * SCALE)
        tops, totals = keep(spans, k, acc * a + acc_n * b, tops, totals, best, total * a + total_n * b)
    self_top[spans] = tops
    self_total[spans] = totals

    @pl.loop(1, n)
    def _(d):
        source = lax.rem(me - d + n, n)
        m_copy(d, at(d)).wait_recv()
        q_copy(d, at(d)).wait_recv()
        chunk(r_send, d)
        r_copy(d, source).start()

    @pl.loop(1, n)
    def _(d):
        source = lax.rem(me - d + n, n)
        m_copy(d, at(d)).wait_send()
        q_copy(d, at(d)).wait_send()
        r_copy(d, source).wait_recv()

    live_row = lax.broadcasted_iota(jnp.int32, (rows, 128), 0)

    @pl.loop(0, spans)
    def _(j):
        back = back_ref[j]
        got = r_recv[back]
        top, total = unpack_stats(got[:, width:])
        own = self_top[j]
        best = jnp.maximum(top, own)
        a = jnp.exp((top - best) * SCALE)
        b = jnp.exp((own - best) * SCALE)
        share = total * a + self_total[j] * b
        live = live_row < length_ref[j]
        share = jnp.where(lane < heads * sharing, share, 1.0)
        a = jnp.where(live, a / share, 0.0)
        b = jnp.where(live, b / share, 0.0)
        for h in range(heads * sharing):
            cols = slice(h * HD, (h + 1) * HD)
            out = got[:, cols].astype(jnp.float32) * a[:, h : h + 1] + self_acc[j, :, cols] * b[:, h : h + 1]
            prefill_out[j, :, cols] = out.astype(jnp.bfloat16)

    @pl.loop(0, n)
    def _(d):
        got = r_recv[d * per + cap]
        top, total = unpack_stats(got[:, width:])
        own = self_top[spans]
        best = jnp.maximum(top, own)
        a = jnp.exp((top - best) * SCALE)
        b = jnp.exp((own - best) * SCALE)
        for h in range(heads * sharing):
            cols = slice(h * HD, (h + 1) * HD)
            self_acc[spans, :, cols] = (
                got[:, cols].astype(jnp.float32) * a[:, h : h + 1]
                + self_acc[spans, :, cols] * b[:, h : h + 1]
            )
        self_total[spans] = total * a + self_total[spans] * b
        self_top[spans] = best

    share = self_total[spans]
    for h in range(heads * sharing):
        cols = slice(h * HD, (h + 1) * HD)
        decode_out[:, cols] = (self_acc[spans, :, cols] / share[:, h : h + 1]).astype(jnp.bfloat16)

    @pl.loop(1, n)
    def _(d):
        r_copy(d, lax.rem(me - d + n, n)).wait_send()


def on_device(
    span_q, span_kv, span_offset, span_length, span_dest, prefix_kv,
    resident_kv, seq_length, decode_q, decode_kv, block_target,
):
    n = lax.axis_size("pool")
    me = lax.axis_index("pool")
    spans, rows, width = span_q.shape
    kv_width = span_kv.shape[-1]
    heads = kv_width // HD
    sharing = width // kv_width
    seqs, steps = decode_q.shape[:2]
    blocks, _, block_len, _ = prefix_kv.shape
    cap = -(-spans // n)
    per = cap + 1
    cap_pad = -(-cap // 8) * 8

    shift = lax.rem(span_dest - me + n, n)
    order = jnp.arange(spans, dtype=jnp.int32)
    before = (shift[None, :] == shift[:, None]) & (order[None, :] < order[:, None])
    rank = jnp.sum(before.astype(jnp.int32), axis=1)
    placed = shift * cap + rank
    back = shift * per + rank
    slots = jnp.arange(n * cap, dtype=jnp.int32)
    source = jnp.sum(jnp.where(placed[None, :] == slots[:, None], order[None, :], 0), axis=1)
    targets = jnp.repeat(block_target, block_len)[None, :]
    decode_pair = jnp.transpose(decode_kv, (1, 0, 2, 3)).reshape(2, seqs * steps, kv_width)
    decode_rows = decode_q.reshape(seqs * steps, width)

    bf = jnp.bfloat16
    smem = pl.BlockSpec(memory_space=pltpu.SMEM)
    vmem = pl.BlockSpec(memory_space=pltpu.VMEM)
    hbm = pl.BlockSpec(memory_space=pl.ANY)
    prefill_out, decode_out = pl.pallas_call(
        functools.partial(kernel, n, cap, rows, heads, sharing, steps),
        out_shape=(
            jax.ShapeDtypeStruct((spans, rows, width), bf),
            jax.ShapeDtypeStruct((seqs * steps, width), bf),
        ),
        in_specs=[smem] * 5 + [vmem, vmem, hbm, hbm, hbm, vmem, vmem],
        out_specs=(vmem, vmem),
        scratch_shapes=[
            pltpu.VMEM((heads, blocks, block_len, HD), bf),
            pltpu.VMEM((heads, blocks, block_len, HD), bf),
            pltpu.VMEM(resident_kv.shape, bf),
            pltpu.VMEM(span_kv.shape, bf),
            pltpu.VMEM((n * per, rows, width), bf),
            pltpu.VMEM((n * per, rows, width), bf),
            pltpu.VMEM((n, cap_pad, 128), jnp.int32),
            pltpu.VMEM((n, cap_pad, 128), jnp.int32),
            pltpu.VMEM((n * per, rows, width + 128), bf),
            pltpu.VMEM((n * per, rows, width + 128), bf),
            pltpu.VMEM((spans + 1, rows, width), jnp.float32),
            pltpu.VMEM((spans + 1, rows, 128), jnp.float32),
            pltpu.VMEM((spans + 1, rows, 128), jnp.float32),
        ]
        + [pltpu.SemaphoreType.DMA((n,))] * 6
        + [pltpu.SemaphoreType.DMA((2 * heads + 2,))],
        compiler_params=pltpu.CompilerParams(
            collective_id=0, has_side_effects=True, vmem_limit_bytes=56 * 2**20
        ),
        cost_estimate=pl.CostEstimate(
            flops=4 * (spans + cap) * rows * width * blocks * block_len,
            bytes_accessed=12 * 2**20,
            transcendentals=(spans + cap) * rows * heads * sharing * blocks * block_len,
        ),
    )(
        source, back, span_offset, span_length, seq_length,
        targets, span_q, span_kv, prefix_kv, resident_kv, decode_rows, decode_pair,
    )
    return prefill_out, decode_out.reshape(seqs, steps, width)


def solution(mesh):
    return jax.shard_map(
        on_device,
        mesh=mesh,
        in_specs=(
            P(("groups", "pool"), None, "tp"),
            P(("groups", "pool"), None, None, "tp"),
            P(("groups", "pool")),
            P(("groups", "pool")),
            P(("groups", "pool")),
            P(("groups", "pool"), None, None, "tp"),
            P(("groups", "pool"), None, None, "tp"),
            P(("groups", "pool")),
            P(("groups", "pool"), None, "tp"),
            P(("groups", "pool"), None, None, "tp"),
            P(("groups", "pool")),
        ),
        out_specs=(P(("groups", "pool"), None, "tp"), P(("groups", "pool"), None, "tp")),
        check_vma=False,
    )
```

time: 177 us -> 86.8 us (0.49)
  Pallas kernels: 0 us -> 75 us
  waiting for transfers between devices: 46 us -> 0 us
  local copies, waits for them, and re-layouts: 50.7 us -> 8.01 us
  starting transfers between devices: 28.5 us -> 0 us
  other arithmetic: 26.4 us -> 2.78 us
  matrix products: 22.6 us -> 0 us
    pallas_call x0 -> x1, Pallas kernels: none -> 75 us  [on_device(): pl.pallas_call(functools.partial(kernel, n, cap, rows, heads, sharing, st...]
    all_to_all x6 -> x0, waiting for transfers between devices: 46 us -> none  [the longest x1 20.5 us: on_device(): lax.all_to_all(send_q, 'pool', split_axis=0, concat_axis=0, tiled=True)]
    all_to_all x6 -> x0, starting transfers between devices: 28.5 us -> none  [the longest x1 6.32 us: on_device(): lax.all_to_all(slot_target, 'pool', split_axis=0, concat_axis=0, tiled=True)]
    dot_general x24 -> x0, matrix products: 22.6 us -> none  [the longest x4 5.03 us: span_attention(): jnp.einsum('rikgd,jkd->rkgij', query_block, prefix_keys, preferred_elemen...]
    sub x8 -> x0, other arithmetic: 13.7 us -> none  [the longest x4 13.7 us: softmax_parts(): expons = jnp.where(allowed, jnp.exp(masked - highest[..., None]), 0.0)]
    gather x7 -> x0, local copies, waits for them, and re-layouts: 10.3 us -> none  [the longest x1 2.46 us: on_device(): jnp.take(span_kv, picked, axis=0)]
    slice x3 -> x0, local copies, waits for them, and re-layouts: 9.37 us -> none  [the longest x1 4.55 us: on_device(): res_values = resident_kv[:, 1].reshape(seqs_here, -1, heads, HD)]
    select_n x16 -> x0, other arithmetic: 7.5 us -> none  [the longest x1 2.47 us: on_device(): jnp.where(filled[:, None, None], jnp.take(span_q, picked, axis=0), jnp.ze...]
  transfers between devices with their start and end apart: 6 -> 0, of which waited for: 5 -> 0; matrix products, arithmetic and copies ran while one was open for 52% -> 0% of each run, Pallas kernels for 0% -> 0%
where the time goes in v1:
time: 86.8 us; the launch traced here: 86.4 us
  Pallas kernels  75 us (86%)
  local copies, waits for them, and re-layouts  8.01 us (9%)
  other arithmetic  2.78 us (3%)
    pallas_call x1, Pallas kernels, on_device(): pl.pallas_call(functools.partial(kernel, n, cap, rows, heads, sharing, st...  75 us
    unnamed x1, local copies, waits for them, and re-layouts  2.29 us

profile of v1, /device:TPU:0, one launch (start us, length us, event | category | flops | bytes accessed | tf_op | source)
XLA Modules:
  0.0 86.4 jit_solution(7400328337695530821)
XLA Ops:
  0.6 0.7 compare_select_fusion
  1.3 0.2 convert_reduce_fusion
  1.5 1.2 %multiply_add_fusion = (s32[16]{0:T(128)}, s32[16]{0:T(128)S(1)}) fusion(s32[16]{0:T(128)S(1)} %convert_reduce_fusion, s32[16]{0:T(128)} %param.15, s32[]{:T(128)S(6)} %axis_index.15), kind=kLoop, calls=%fused_computation.8 | loop fusion | flops 192 | bytes 260 | tf_op jit(solution)/shard_map/add | solution.py:320
  2.7 0.7 select_reduce_fusion.from_ref
  3.4 1.3 %broadcast_in_dim.9 = s32[16,128]{1,0:T(8,128)} broadcast(s32[16]{0:T(128)} %param.21), dimensions={0} | broadcast | bytes 8256 | tf_op jit(solution)/shard_map/broadcast_in_dim | solution.py:323
  4.7 0.8 copy.14
  5.5 0.6 reshape.17.decode_kv
  6.2 1.5 %reshape.16.decode_q = bf16[32,1024]{1,0:T(8,128)(2,1)} reshape(bf16[8,4,1024]{2,1,0:T(4,128)(2,1)} %param.19) | data formatting | bytes 131072 | tf_op jit(solution)/shard_map/reshape | solution.py:325
  7.6 75.0 %shard_map.122 = (bf16[16,32,1024]{2,1,0:T(8,128)(2,1)}, bf16[32,1024]{1,0:T(8,128)(2,1)}) custom-call(s32[16]{0:T(128)} %select_reduce_fusion.from_ref, s32[16]{0:T(128)} %get-tuple-element.6.back_ref, s32[16]{0:T(128)} %offset_ref.1, s32[16]{0:T(128)} %length_ref.1, s32[8]{0:T(128)} %seqlen_ref.1, s32[1,2048]{1,0:T(1,128)} %bitcast.3, ...), custom_call_target="tpu_custom_call" | custom-call | flops 5368709120 | bytes 12582912 | tf_op jit(solution)/shard_map/pallas_call | solution.py:331
  82.6 1.5 %reshape.18 = bf16[8,4,1024]{2,1,0:T(4,128)(2,1)} reshape(bf16[32,1024]{1,0:T(8,128)(2,1)} %get-tuple-element.5) | data formatting | bytes 131072 | tf_op jit(solution)/shard_map/reshape | solution.py:368
  84.1 2.3 %copy.16 = bf16[16,32,1024]{2,1,0:T(8,128)(2,1)} copy(bf16[16,32,1024]{2,1,0:T(8,128)(2,1)} %get-tuple-element.10) | data formatting | bytes 2097152

commit v2 on v1

--- a/solution.py
+++ b/solution.py
@@ -10,31 +10,8 @@
 HD = 128
 SCALE = HD ** (-0.5)
 LOW = -1e30
-GAP = 16
 NT = (((1,), (1,)), ((), ()))
 NN = (((1,), (0,)), ((), ()))
-
-
-def split_bf16(x):
-    high = x.astype(jnp.bfloat16).astype(jnp.float32)
-    rest = x - high
-    mid = rest.astype(jnp.bfloat16).astype(jnp.float32)
-    return high, mid, rest - mid
-
-
-def pack_stats(top, total):
-    a, b, c = split_bf16(top)
-    d, e, _ = split_bf16(total)
-    out = a + pltpu.roll(b, GAP, 1) + pltpu.roll(c, 2 * GAP, 1)
-    out = out + pltpu.roll(d, 3 * GAP, 1) + pltpu.roll(e, 4 * GAP, 1)
-    return out.astype(jnp.bfloat16)
-
-
-def unpack_stats(packed):
-    t = packed.astype(jnp.float32)
-    top = t + pltpu.roll(t, 128 - GAP, 1) + pltpu.roll(t, 128 - 2 * GAP, 1)
-    total = pltpu.roll(t, 128 - 3 * GAP, 1) + pltpu.roll(t, 128 - 4 * GAP, 1)
-    return top, total
 
 
 def soft(scores):
@@ -45,12 +22,12 @@
 
 def kernel(
     n, cap, rows, heads, sharing, steps,
-    from_ref, back_ref, offset_ref, length_ref, seqlen_ref,
-    target_ref, span_q, span_kv, prefix, resident, decode_q, decode_kv,
+    dest_ref, offset_ref, length_ref, seqlen_ref, target_ref,
+    span_q, span_kv, prefix, resident, step_q, step_kv,
     prefill_out, decode_out,
     keys, values, res, own_kv, q_send, q_recv, m_send, m_recv, r_send, r_recv,
-    self_acc, self_top, self_total,
-    q_ssem, q_rsem, m_ssem, m_rsem, r_ssem, r_rsem, loc_sem,
+    t_send, t_recv, self_acc, self_top, self_total, target_row, decode_q, decode_pair, new_kv,
+    q_ssem, q_rsem, m_ssem, m_rsem, r_ssem, r_rsem, t_ssem, t_rsem, loc_sem,
 ):
     me = lax.axis_index("pool")
     spans = span_q.shape[0]
@@ -58,6 +35,8 @@
     per = cap + 1
     width = heads * sharing * HD
     tall = sharing * rows
+    count = heads * sharing
+    block_len = prefix.shape[2]
 
     def at(step):
         return lax.rem(me + step, n)
@@ -80,10 +59,28 @@
     def _(d):
         pl.semaphore_signal(barrier, inc=1, device_id={"pool": at(d)}, device_id_type=pl.DeviceIdType.MESH)
 
+    def shift_of(j):
+        away = dest_ref[j] - me
+        return jnp.where(away < 0, away + n, away)
+
+    def span_at(d, r):
+        pick = seen = jnp.int32(0)
+        for j in range(spans):
+            hit = shift_of(j) == d
+            pick = jnp.where(hit & (seen == r), j, pick)
+            seen = seen + hit.astype(jnp.int32)
+        return pick
+
+    def rank_of(j):
+        rank = jnp.int32(0)
+        for i in range(spans):
+            rank = rank + ((dest_ref[i] == dest_ref[j]) & (i < j)).astype(jnp.int32)
+        return jnp.minimum(rank, cap - 1)
+
     def fill(buf, meta, d):
         @pl.loop(0, cap)
         def _(r):
-            pick = from_ref[d * cap + r]
+            pick = span_at(d, r)
             buf[d * per + r] = span_q[pick]
             meta[d, pl.ds(r, 1), :] = jnp.full((1, 128), offset_ref[pick], jnp.int32)
 
@@ -104,6 +101,17 @@
             device_id={"pool": to}, device_id_type=pl.DeviceIdType.MESH,
         )
 
+    def t_copy(d, to):
+        return pltpu.make_async_remote_copy(
+            src_ref=t_send.at[d], dst_ref=t_recv.at[d],
+            send_sem=t_ssem.at[d], recv_sem=t_rsem.at[d],
+            device_id={"pool": to}, device_id_type=pl.DeviceIdType.MESH,
+        )
+
+    def near(i):
+        odd = lax.rem(i, 2)
+        return odd * ((i + 1) // 2) + (1 - odd) * (n - i // 2)
+
     def r_copy(d, to):
         return pltpu.make_async_remote_copy(
             src_ref=r_send.at[pl.ds(d * per, per)],
@@ -112,17 +120,26 @@
             device_id={"pool": to}, device_id_type=pl.DeviceIdType.MESH,
         )
 
+    for s in range(seqs):
+        part = slice(s * steps, (s + 1) * steps)
+        decode_pair[part, :] = step_q[s].astype(jnp.float32)
+        for k in range(2):
+            new_kv[k, part, :] = step_kv[s, k].astype(jnp.float32)
+    decode_q[...] = decode_pair[...].astype(jnp.bfloat16)
     m_send[...] = jnp.zeros_like(m_send)
     m_recv[0] = jnp.zeros(m_recv.shape[1:], jnp.int32)
     pl.semaphore_wait(barrier, n - 1)
 
     @pl.loop(1, n)
-    def _(d):
+    def _(i):
+        d = near(i)
         fill(q_send, m_send, d)
         m_copy(d, at(d)).start()
         q_copy(d, at(d)).start()
 
     fill(q_recv, m_recv, 0)
+    for b in range(prefix.shape[0]):
+        target_row[:, b * block_len : (b + 1) * block_len] = jnp.full((8, block_len), target_ref[b], jnp.int32)
 
     lane = lax.broadcasted_iota(jnp.int32, (rows, 128), 1)
 
@@ -140,9 +157,10 @@
             totals = jnp.where(lane == h, total[part], totals)
         return tops, totals
 
-    def attend(buf, out, slot, bias):
+    def attend(buf, out, stats, d, r, bias):
+        slot = d * per + r
         block = buf[slot]
-        tops = totals = jnp.zeros((rows, 128), jnp.float32)
+        tile = stats[d]
         for k in range(heads):
             query = stacked(block, k)
             key = keys[k].reshape(-1, HD)
@@ -157,25 +175,41 @@
             for g in range(sharing):
                 h = k * sharing + g
                 out[slot, :, h * HD : (h + 1) * HD] = acc[g * rows : (g + 1) * rows].astype(jnp.bfloat16)
-            tops, totals = spread(tops, totals, top, total, k)
-        out[slot, :, width:] = pack_stats(tops, totals)
+            for g in range(sharing):
+                part = slice(g * rows, (g + 1) * rows)
+                spot = r * 2 * count + k * sharing + g
+                tile = jnp.where(lane == spot, top[part], tile)
+                tile = jnp.where(lane == spot + count, total[part], tile)
+        stats[d] = tile
 
     tokens = keys.shape[1] * keys.shape[2]
     position = lax.broadcasted_iota(jnp.int32, (1, tokens), 1)
 
-    def chunk(out, d):
+    def chunk(out, stats, d):
+        stats[d] = jnp.zeros((rows, 128), jnp.float32)
+
         @pl.loop(0, cap)
         def _(r):
             limit = m_recv[d, pl.ds(r, 1), :][:, :1]
-            attend(q_recv, out, d * per + r, jnp.where(position < limit, 0.0, LOW))
+            attend(q_recv, out, stats, d, r, jnp.where(position < limit, 0.0, LOW))
 
         source = lax.rem(me - d + n, n)
         seq = source * seqs + lax.broadcasted_iota(jnp.int32, (rows, 1), 0) // steps
-        attend(q_recv, out, d * per + cap, jnp.where(target_ref[...] == seq, 0.0, LOW))
+        attend(q_recv, out, stats, d, cap, jnp.where(target_row[0:1, :] == seq, 0.0, LOW))
 
     for load in loads:
         load.wait()
-    chunk(r_recv, 0)
+    chunk(r_recv, t_recv, 0)
+
+    @pl.loop(1, n)
+    def _(i):
+        d = near(i)
+        source = lax.rem(me - d + n, n)
+        m_copy(d, at(d)).wait_recv()
+        q_copy(d, at(d)).wait_recv()
+        chunk(r_send, t_send, d)
+        t_copy(d, source).start()
+        r_copy(d, source).start()
 
     own_load.wait()
     row_of = lax.rem(lax.broadcasted_iota(jnp.int32, (tall, rows), 0), rows)
@@ -222,10 +256,10 @@
 
         zero = jnp.zeros((tall, 1), jnp.float32)
         acc, top, total = lax.fori_loop(0, seqs, one, (jnp.zeros((tall, HD), jnp.float32), zero, zero))
-        score = lax.dot_general(query, decode_kv[0, :, cols], NT, preferred_element_type=jnp.float32)
+        score = lax.dot_general(query, new_kv[0, :, cols].astype(jnp.bfloat16), NT, preferred_element_type=jnp.float32)
         fits = (col_of // steps == row_of // steps) & (col_of <= row_of)
         top_n, weight, total_n = soft(jnp.where(fits, score, LOW))
-        acc_n = lax.dot_general(weight, decode_kv[1, :, cols], NN, preferred_element_type=jnp.float32)
+        acc_n = lax.dot_general(weight, new_kv[1, :, cols].astype(jnp.bfloat16), NN, preferred_element_type=jnp.float32)
         best = jnp.maximum(top, top_n)
         a = jnp.exp((top - best) * SCALE)
         b = jnp.exp((top_n - best) * SCALE)
@@ -236,32 +270,32 @@
     @pl.loop(1, n)
     def _(d):
         source = lax.rem(me - d + n, n)
-        m_copy(d, at(d)).wait_recv()
-        q_copy(d, at(d)).wait_recv()
-        chunk(r_send, d)
-        r_copy(d, source).start()
-
-    @pl.loop(1, n)
-    def _(d):
-        source = lax.rem(me - d + n, n)
         m_copy(d, at(d)).wait_send()
         q_copy(d, at(d)).wait_send()
+        t_copy(d, source).wait_recv()
         r_copy(d, source).wait_recv()
+
+    def stats_of(tile, rank):
+        top = tile
+        for r in range(1, per):
+            top = jnp.where(rank == r, pltpu.roll(tile, 128 - r * 2 * count, 1), top)
+        return top, pltpu.roll(top, 128 - count, 1)
 
     live_row = lax.broadcasted_iota(jnp.int32, (rows, 128), 0)
 
     @pl.loop(0, spans)
     def _(j):
-        back = back_ref[j]
-        got = r_recv[back]
-        top, total = unpack_stats(got[:, width:])
+        away = shift_of(j)
+        rank = rank_of(j)
+        got = r_recv[away * per + rank]
+        top, total = stats_of(t_recv[away], rank)
         own = self_top[j]
         best = jnp.maximum(top, own)
         a = jnp.exp((top - best) * SCALE)
         b = jnp.exp((own - best) * SCALE)
         share = total * a + self_total[j] * b
         live = live_row < length_ref[j]
-        share = jnp.where(lane < heads * sharing, share, 1.0)
+        share = jnp.where(lane < count, share, 1.0)
         a = jnp.where(live, a / share, 0.0)
         b = jnp.where(live, b / share, 0.0)
         for h in range(heads * sharing):
@@ -272,7 +306,7 @@
     @pl.loop(0, n)
     def _(d):
         got = r_recv[d * per + cap]
-        top, total = unpack_stats(got[:, width:])
+        top, total = stats_of(t_recv[d], cap)
         own = self_top[spans]
         best = jnp.maximum(top, own)
         a = jnp.exp((top - best) * SCALE)
@@ -287,12 +321,15 @@
         self_top[spans] = best
 
     share = self_total[spans]
-    for h in range(heads * sharing):
+    for h in range(count):
         cols = slice(h * HD, (h + 1) * HD)
-        decode_out[:, cols] = (self_acc[spans, :, cols] / share[:, h : h + 1]).astype(jnp.bfloat16)
+        decode_pair[:, cols] = self_acc[spans, :, cols] / share[:, h : h + 1]
+    for s in range(seqs):
+        decode_out[s] = decode_pair[s * steps : (s + 1) * steps, :].astype(jnp.bfloat16)
 
     @pl.loop(1, n)
     def _(d):
+        t_copy(d, lax.rem(me - d + n, n)).wait_send()
         r_copy(d, lax.rem(me - d + n, n)).wait_send()
 
 
@@ -301,7 +338,6 @@
     resident_kv, seq_length, decode_q, decode_kv, block_target,
 ):
     n = lax.axis_size("pool")
-    me = lax.axis_index("pool")
     spans, rows, width = span_q.shape
     kv_width = span_kv.shape[-1]
     heads = kv_width // HD
@@ -312,18 +348,6 @@
     per = cap + 1
     cap_pad = -(-cap // 8) * 8
 
-    shift = lax.rem(span_dest - me + n, n)
-    order = jnp.arange(spans, dtype=jnp.int32)
-    before = (shift[None, :] == shift[:, None]) & (order[None, :] < order[:, None])
-    rank = jnp.sum(before.astype(jnp.int32), axis=1)
-    placed = shift * cap + rank
-    back = shift * per + rank
-    slots = jnp.arange(n * cap, dtype=jnp.int32)
-    source = jnp.sum(jnp.where(placed[None, :] == slots[:, None], order[None, :], 0), axis=1)
-    targets = jnp.repeat(block_target, block_len)[None, :]
-    decode_pair = jnp.transpose(decode_kv, (1, 0, 2, 3)).reshape(2, seqs * steps, kv_width)
-    decode_rows = decode_q.reshape(seqs * steps, width)
-
     bf = jnp.bfloat16
     smem = pl.BlockSpec(memory_space=pltpu.SMEM)
     vmem = pl.BlockSpec(memory_space=pltpu.VMEM)
@@ -332,9 +356,9 @@
         functools.partial(kernel, n, cap, rows, heads, sharing, steps),
         out_shape=(
             jax.ShapeDtypeStruct((spans, rows, width), bf),
-            jax.ShapeDtypeStruct((seqs * steps, width), bf),
+            jax.ShapeDtypeStruct((seqs, steps, width), bf),
         ),
-        in_specs=[smem] * 5 + [vmem, vmem, hbm, hbm, hbm, vmem, vmem],
+        in_specs=[smem] * 5 + [vmem, hbm, hbm, hbm, vmem, vmem],
         out_specs=(vmem, vmem),
         scratch_shapes=[
             pltpu.VMEM((heads, blocks, block_len, HD), bf),
@@ -345,13 +369,19 @@
             pltpu.VMEM((n * per, rows, width), bf),
             pltpu.VMEM((n, cap_pad, 128), jnp.int32),
             pltpu.VMEM((n, cap_pad, 128), jnp.int32),
-            pltpu.VMEM((n * per, rows, width + 128), bf),
-            pltpu.VMEM((n * per, rows, width + 128), bf),
+            pltpu.VMEM((n * per, rows, width), bf),
+            pltpu.VMEM((n * per, rows, width), bf),
+            pltpu.VMEM((n, rows, 128), jnp.float32),
+            pltpu.VMEM((n, rows, 128), jnp.float32),
             pltpu.VMEM((spans + 1, rows, width), jnp.float32),
             pltpu.VMEM((spans + 1, rows, 128), jnp.float32),
             pltpu.VMEM((spans + 1, rows, 128), jnp.float32),
+            pltpu.VMEM((8, blocks * block_len), jnp.int32),
+            pltpu.VMEM((rows, width), bf),
+            pltpu.VMEM((rows, width), jnp.float32),
+            pltpu.VMEM((2, rows, kv_width), jnp.float32),
         ]
-        + [pltpu.SemaphoreType.DMA((n,))] * 6
+        + [pltpu.SemaphoreType.DMA((n,))] * 8
         + [pltpu.SemaphoreType.DMA((2 * heads + 2,))],
         compiler_params=pltpu.CompilerParams(
             collective_id=0, has_side_effects=True, vmem_limit_bytes=56 * 2**20
@@ -362,10 +392,10 @@
             transcendentals=(spans + cap) * rows * heads * sharing * blocks * block_len,
         ),
     )(
-        source, back, span_offset, span_length, seq_length,
-        targets, span_q, span_kv, prefix_kv, resident_kv, decode_rows, decode_pair,
+        span_dest, span_offset, span_length, seq_length, block_target,
+        span_q, span_kv, prefix_kv, resident_kv, decode_q, decode_kv,
     )
-    return prefill_out, decode_out.reshape(seqs, steps, width)
+    return prefill_out, decode_out
 
 
 def solution(mesh):

time: 86.8 us -> 82.2 us (0.947)
  the two profiles are of different devices: /device:TPU:0 before, /device:TPU:22 now
where the time goes in v2:
time: 82.2 us; the launch traced here: 82 us
  Pallas kernels  77.5 us (94%)
  local copies, waits for them, and re-layouts  3.78 us (5%)
    pallas_call x1, Pallas kernels, on_device(): pl.pallas_call(functools.partial(kernel, n, cap, rows, heads, sharing, st...  77.5 us
    unnamed x2, local copies, waits for them, and re-layouts  3.78 us

profile of v2, /device:TPU:22, one launch (start us, length us, event | category | flops | bytes accessed | tf_op | source)
XLA Modules:
  0.0 82.0 jit_solution(13844261366211810126)
XLA Ops:
  0.6 77.5 %shard_map.122 = (bf16[16,32,1024]{2,1,0:T(8,128)(2,1)}, bf16[8,4,1024]{2,1,0:T(4,128)(2,1)}) custom-call(s32[16]{0:T(128)} %dest_ref.1, s32[16]{0:T(128)} %offset_ref.1, s32[16]{0:T(128)} %length_ref.1, s32[8]{0:T(128)} %seqlen_ref.1, s32[16]{0:T(128)} %target_ref.1, bf16[16,32,1024]{2,1,0:T(8,128)(2,1)} %span_q.1, bf16[16,2,32,256]{3,2,1,0:T(8,128)(2,1)} %span_kv.1, ...), custom_call_target="tpu_custom_call" | custom-call | flops 5368709120 | bytes 12582912 | tf_op jit(solution)/shard_map/pallas_call | solution.py:355
  78.2 2.3 %copy.15 = bf16[16,32,1024]{2,1,0:T(8,128)(2,1)} copy(bf16[16,32,1024]{2,1,0:T(8,128)(2,1)} %get-tuple-element.4) | data formatting | bytes 2097152
  80.5 1.5 %copy.16 = bf16[8,4,1024]{2,1,0:T(4,128)(2,1)} copy(bf16[8,4,1024]{2,1,0:T(4,128)(2,1)} %get-tuple-element.5) | data formatting | bytes 131072

commit v3 on v2

--- a/solution.py
+++ b/solution.py
@@ -77,20 +77,25 @@
             rank = rank + ((dest_ref[i] == dest_ref[j]) & (i < j)).astype(jnp.int32)
         return jnp.minimum(rank, cap - 1)
 
-    def fill(buf, meta, d):
+    def fill(buf, meta, d, send):
         @pl.loop(0, cap)
         def _(r):
             pick = span_at(d, r)
             buf[d * per + r] = span_q[pick]
             meta[d, pl.ds(r, 1), :] = jnp.full((1, 128), offset_ref[pick], jnp.int32)
+            if send:
+                q_copy(d, r, at(d)).start()
 
         buf[d * per + cap] = decode_q[...]
-
-    def q_copy(d, to):
+        if send:
+            m_copy(d, at(d)).start()
+            q_copy(d, cap, at(d)).start()
+
+    def q_copy(d, r, to):
         return pltpu.make_async_remote_copy(
-            src_ref=q_send.at[pl.ds(d * per, per)],
-            dst_ref=q_recv.at[pl.ds(d * per, per)],
-            send_sem=q_ssem.at[d], recv_sem=q_rsem.at[d],
+            src_ref=q_send.at[d * per + r],
+            dst_ref=q_recv.at[d * per + r],
+            send_sem=q_ssem.at[d * per + r], recv_sem=q_rsem.at[d * per + r],
             device_id={"pool": to}, device_id_type=pl.DeviceIdType.MESH,
         )
 
@@ -112,11 +117,11 @@
         odd = lax.rem(i, 2)
         return odd * ((i + 1) // 2) + (1 - odd) * (n - i // 2)
 
-    def r_copy(d, to):
+    def r_copy(d, r, to):
         return pltpu.make_async_remote_copy(
-            src_ref=r_send.at[pl.ds(d * per, per)],
-            dst_ref=r_recv.at[pl.ds(d * per, per)],
-            send_sem=r_ssem.at[d], recv_sem=r_rsem.at[d],
+            src_ref=r_send.at[d * per + r],
+            dst_ref=r_recv.at[d * per + r],
+            send_sem=r_ssem.at[d * per + r], recv_sem=r_rsem.at[d * per + r],
             device_id={"pool": to}, device_id_type=pl.DeviceIdType.MESH,
         )
 
@@ -133,11 +138,9 @@
     @pl.loop(1, n)
     def _(i):
         d = near(i)
-        fill(q_send, m_send, d)
-        m_copy(d, at(d)).start()
-        q_copy(d, at(d)).start()
-
-    fill(q_recv, m_recv, 0)
+        fill(q_send, m_send, d, True)
+
+    fill(q_recv, m_recv, 0, False)
     for b in range(prefix.shape[0]):
         target_row[:, b * block_len : (b + 1) * block_len] = jnp.full((8, block_len), target_ref[b], jnp.int32)
 
@@ -185,31 +188,36 @@
     tokens = keys.shape[1] * keys.shape[2]
     position = lax.broadcasted_iota(jnp.int32, (1, tokens), 1)
 
-    def chunk(out, stats, d):
+    def chunk(out, stats, d, away):
+        source = lax.rem(me - d + n, n)
         stats[d] = jnp.zeros((rows, 128), jnp.float32)
 
         @pl.loop(0, cap)
         def _(r):
+            if away:
+                q_copy(d, r, at(d)).wait_recv()
             limit = m_recv[d, pl.ds(r, 1), :][:, :1]
             attend(q_recv, out, stats, d, r, jnp.where(position < limit, 0.0, LOW))
-
-        source = lax.rem(me - d + n, n)
+            if away:
+                r_copy(d, r, source).start()
+
+        if away:
+            q_copy(d, cap, at(d)).wait_recv()
         seq = source * seqs + lax.broadcasted_iota(jnp.int32, (rows, 1), 0) // steps
         attend(q_recv, out, stats, d, cap, jnp.where(target_row[0:1, :] == seq, 0.0, LOW))
+        if away:
+            r_copy(d, cap, source).start()
+            t_copy(d, source).start()
 
     for load in loads:
         load.wait()
-    chunk(r_recv, t_recv, 0)
+    chunk(r_recv, t_recv, 0, False)
 
     @pl.loop(1, n)
     def _(i):
         d = near(i)
-        source = lax.rem(me - d + n, n)
         m_copy(d, at(d)).wait_recv()
-        q_copy(d, at(d)).wait_recv()
-        chunk(r_send, t_send, d)
-        t_copy(d, source).start()
-        r_copy(d, source).start()
+        chunk(r_send, t_send, d, True)
 
     own_load.wait()
     row_of = lax.rem(lax.broadcasted_iota(jnp.int32, (tall, rows), 0), rows)
@@ -271,9 +279,12 @@
     def _(d):
         source = lax.rem(me - d + n, n)
         m_copy(d, at(d)).wait_send()
-        q_copy(d, at(d)).wait_send()
         t_copy(d, source).wait_recv()
-        r_copy(d, source).wait_recv()
+
+        @pl.loop(0, per)
+        def _(r):
+            q_copy(d, r, at(d)).wait_send()
+            r_copy(d, r, source).wait_recv()
 
     def stats_of(tile, rank):
         top = tile
@@ -330,7 +341,10 @@
     @pl.loop(1, n)
     def _(d):
         t_copy(d, lax.rem(me - d + n, n)).wait_send()
-        r_copy(d, lax.rem(me - d + n, n)).wait_send()
+
+        @pl.loop(0, per)
+        def _(r):
+            r_copy(d, r, lax.rem(me - d + n, n)).wait_send()
 
 
 def on_device(
@@ -381,7 +395,10 @@
             pltpu.VMEM((rows, width), jnp.float32),
             pltpu.VMEM((2, rows, kv_width), jnp.float32),
         ]
-        + [pltpu.SemaphoreType.DMA((n,))] * 8
+        + [pltpu.SemaphoreType.DMA((n * per,))] * 2
+        + [pltpu.SemaphoreType.DMA((n,))] * 2
+        + [pltpu.SemaphoreType.DMA((n * per,))] * 2
+        + [pltpu.SemaphoreType.DMA((n,))] * 2
         + [pltpu.SemaphoreType.DMA((2 * heads + 2,))],
         compiler_params=pltpu.CompilerParams(
             collective_id=0, has_side_effects=True, vmem_limit_bytes=56 * 2**20

time: 82.2 us -> 78.2 us (0.951)
  the two profiles are of different devices: /device:TPU:22 before, /device:TPU:0 now
where the time goes in v3:
time: 78.2 us; the launch traced here: 78 us
  Pallas kernels  73.6 us (94%)
  local copies, waits for them, and re-layouts  3.78 us (5%)
    pallas_call x1, Pallas kernels, on_device(): pl.pallas_call(functools.partial(kernel, n, cap, rows, heads, sharing, st...  73.6 us
    unnamed x2, local copies, waits for them, and re-layouts  3.78 us

profile of v3, /device:TPU:0, one launch (start us, length us, event | category | flops | bytes accessed | tf_op | source)
XLA Modules:
  0.0 78.0 jit_solution(8467303521988117148)
XLA Ops:
  0.6 73.6 %shard_map.122 = (bf16[16,32,1024]{2,1,0:T(8,128)(2,1)}, bf16[8,4,1024]{2,1,0:T(4,128)(2,1)}) custom-call(s32[16]{0:T(128)} %dest_ref.1, s32[16]{0:T(128)} %offset_ref.1, s32[16]{0:T(128)} %length_ref.1, s32[8]{0:T(128)} %seqlen_ref.1, s32[16]{0:T(128)} %target_ref.1, bf16[16,32,1024]{2,1,0:T(8,128)(2,1)} %span_q.1, bf16[16,2,32,256]{3,2,1,0:T(8,128)(2,1)} %span_kv.1, ...), custom_call_target="tpu_custom_call" | custom-call | flops 5368709120 | bytes 12582912 | tf_op jit(solution)/shard_map/pallas_call | solution.py:369
  74.2 2.3 %copy.15 = bf16[16,32,1024]{2,1,0:T(8,128)(2,1)} copy(bf16[16,32,1024]{2,1,0:T(8,128)(2,1)} %get-tuple-element.4) | data formatting | bytes 2097152
  76.5 1.5 %copy.16 = bf16[8,4,1024]{2,1,0:T(4,128)(2,1)} copy(bf16[8,4,1024]{2,1,0:T(4,128)(2,1)} %get-tuple-element.5) | data formatting | bytes 131072

commit v4 on v3

--- a/solution.py
+++ b/solution.py
@@ -275,22 +275,43 @@
     self_top[spans] = tops
     self_total[spans] = totals
 
-    @pl.loop(1, n)
-    def _(d):
-        source = lax.rem(me - d + n, n)
-        m_copy(d, at(d)).wait_send()
-        t_copy(d, source).wait_recv()
-
-        @pl.loop(0, per)
-        def _(r):
-            q_copy(d, r, at(d)).wait_send()
-            r_copy(d, r, source).wait_recv()
-
     def stats_of(tile, rank):
         top = tile
         for r in range(1, per):
             top = jnp.where(rank == r, pltpu.roll(tile, 128 - r * 2 * count, 1), top)
         return top, pltpu.roll(top, 128 - count, 1)
+
+    def merge_decode(d):
+        got = r_recv[d * per + cap]
+        top, total = stats_of(t_recv[d], cap)
+        own = self_top[spans]
+        best = jnp.maximum(top, own)
+        a = jnp.exp((top - best) * SCALE)
+        b = jnp.exp((own - best) * SCALE)
+        for h in range(heads * sharing):
+            cols = slice(h * HD, (h + 1) * HD)
+            self_acc[spans, :, cols] = (
+                got[:, cols].astype(jnp.float32) * a[:, h : h + 1]
+                + self_acc[spans, :, cols] * b[:, h : h + 1]
+            )
+        self_total[spans] = total * a + self_total[spans] * b
+        self_top[spans] = best
+
+    merge_decode(0)
+
+    @pl.loop(1, n)
+    def _(i):
+        d = near(i)
+        source = lax.rem(me - d + n, n)
+        m_copy(d, at(d)).wait_send()
+        t_copy(d, source).wait_recv()
+
+        @pl.loop(0, per)
+        def _(r):
+            q_copy(d, r, at(d)).wait_send()
+            r_copy(d, r, source).wait_recv()
+
+        merge_decode(d)
 
     live_row = lax.broadcasted_iota(jnp.int32, (rows, 128), 0)
 
@@ -313,23 +334,6 @@
             cols = slice(h * HD, (h + 1) * HD)
             out = got[:, cols].astype(jnp.float32) * a[:, h : h + 1] + self_acc[j, :, cols] * b[:, h : h + 1]
             prefill_out[j, :, cols] = out.astype(jnp.bfloat16)
-
-    @pl.loop(0, n)
-    def _(d):
-        got = r_recv[d * per + cap]
-        top, total = stats_of(t_recv[d], cap)
-        own = self_top[spans]
-        best = jnp.maximum(top, own)
-        a = jnp.exp((top - best) * SCALE)
-        b = jnp.exp((own - best) * SCALE)
-        for h in range(heads * sharing):
-            cols = slice(h * HD, (h + 1) * HD)
-            self_acc[spans, :, cols] = (
-                got[:, cols].astype(jnp.float32) * a[:, h : h + 1]
-                + self_acc[spans, :, cols] * b[:, h : h + 1]
-            )
-        self_total[spans] = total * a + self_total[spans] * b
-        self_top[spans] = best
 
     share = self_total[spans]
     for h in range(count):

time: 78.2 us -> 77.6 us (level)
  Pallas kernels: 73.6 us -> 72.8 us
where the time goes in v4:
time: 77.6 us; the launch traced here: 77.3 us
  Pallas kernels  72.8 us (94%)
  local copies, waits for them, and re-layouts  3.78 us (5%)
    pallas_call x1, Pallas kernels, on_device(): pl.pallas_call(functools.partial(kernel, n, cap, rows, heads, sharing, st...  72.8 us
    unnamed x2, local copies, waits for them, and re-layouts  3.78 us

profile of v4, /device:TPU:0, one launch (start us, length us, event | category | flops | bytes accessed | tf_op | source)
XLA Modules:
  0.0 77.3 jit_solution(12230257790526988330)
XLA Ops:
  0.6 72.8 %shard_map.122 = (bf16[16,32,1024]{2,1,0:T(8,128)(2,1)}, bf16[8,4,1024]{2,1,0:T(4,128)(2,1)}) custom-call(s32[16]{0:T(128)} %dest_ref.1, s32[16]{0:T(128)} %offset_ref.1, s32[16]{0:T(128)} %length_ref.1, s32[8]{0:T(128)} %seqlen_ref.1, s32[16]{0:T(128)} %target_ref.1, bf16[16,32,1024]{2,1,0:T(8,128)(2,1)} %span_q.1, bf16[16,2,32,256]{3,2,1,0:T(8,128)(2,1)} %span_kv.1, ...), custom_call_target="tpu_custom_call" | custom-call | flops 5368709120 | bytes 12582912 | tf_op jit(solution)/shard_map/pallas_call | solution.py:373
  73.5 2.3 %copy.15 = bf16[16,32,1024]{2,1,0:T(8,128)(2,1)} copy(bf16[16,32,1024]{2,1,0:T(8,128)(2,1)} %get-tuple-element.4) | data formatting | bytes 2097152
  75.8 1.5 %copy.16 = bf16[8,4,1024]{2,1,0:T(4,128)(2,1)} copy(bf16[8,4,1024]{2,1,0:T(4,128)(2,1)} %get-tuple-element.5) | data formatting | bytes 131072
